TPU v7x, 128 devices: a whole 4x4x4 slice. The times are simulated.
128 devices in a mesh: row: 32 (over x, y, core), col: 4 (over z).
Axes of the slice: x: 4, y: 4, z: 4, core: 2. Of those that a mesh axis runs over, the one named last changes fastest.
Arguments:
- tokens: bfloat16 [8192, 1024], P('row', 'col'), may hold values from -6 to 6
- run_counts: int32 [32], replicated, may hold values from 128 to 256, as said below
- seq_lengths: int32 [8], replicated, may hold values from 1 to 8192, as said below
- first_gain: bfloat16 [1024], P('col'), may hold values from 0.099609375 to 1.8984375
- in_weight: bfloat16 [1024, 3, 1024], P('row', None, 'col'), may hold values from -0.1875 to 0.1875
- conv_weight: bfloat16 [3, 1024], P(None, 'col'), may hold values from -3 to 3
- out_weight: bfloat16 [1024, 1024], P('row', 'col'), may hold values from -0.1875 to 0.1875
- second_gain: bfloat16 [1024], P('col'), may hold values from 0.099609375 to 1.8984375
- gate_weight: bfloat16 [1024, 4608], P('row', 'col'), may hold values from -0.1875 to 0.1875
- up_weight: bfloat16 [1024, 4608], P('row', 'col'), may hold values from -0.1875 to 0.1875
- down_weight: bfloat16 [4608, 1024], P('row', 'col'), may hold values from -0.125 to 0.125
- cotangent: bfloat16 [8192, 1024], P('row', 'col'), may hold values from -6 to 6
Outputs:
- block_out: bfloat16 [8192, 1024], P('row', 'col')
- input_grad: float32 [8192, 1024], P('row', 'col')
- first_gain_grad: float32 [1024], P('col')
- in_weight_grad: float32 [1024, 3, 1024], P('row', None, 'col')
- conv_weight_grad: float32 [3, 1024], P(None, 'col')
- out_weight_grad: float32 [1024, 1024], P('row', 'col')
- second_gain_grad: float32 [1024], P('col')
- gate_grad: float32 [1024, 4608], P('row', 'col')
- up_grad: float32 [1024, 4608], P('row', 'col')
- down_grad: float32 [4608, 1024], P('row', 'col')
Inputs may be any that keep to these rules, and one draw needn't show every extreme that they name: `run_counts`: some index of row holds exactly 256 live tokens and another exactly 128. `seq_lengths`: exactly one sequence, at an index that varies, is 8192 long; the sequences before it are together shorter than 128.
All inputs are finite; a program needn't handle non-finite values.
Results may differ from a plain program's by a relative error of at most 0.015.
Values may be sent and summed in bfloat16 or wider, within the bound.
A program may use at most 64 MiB of HBM per device.

v0:
```python
import jax
import jax.numpy as jnp
from jax import lax
from jax.sharding import PartitionSpec as P

epsilon = 1e-05


def passed_along(block, axis, distance):
    devices = range(lax.axis_size(axis))
    route = [(i - distance, i) for i in devices if i - distance in devices]
    return lax.ppermute(block, axis, route)


def fetch_weights(in_weight, out_weight, gate_weight, up_weight, down_weight):
    in_full, out_full, gate_full, up_full, down_full = (
        lax.all_gather(in_weight, "row", axis=0, tiled=True),
        lax.all_gather(out_weight, "row", axis=0, tiled=True),
        lax.all_gather(gate_weight, "row", axis=0, tiled=True),
        lax.all_gather(up_weight, "row", axis=0, tiled=True),
        lax.all_gather(down_weight, "row", axis=0, tiled=True),
    )
    return (in_full, out_full, gate_full, up_full, down_full)


def own_columns(values, col_start, width_local):
    return lax.dynamic_slice_in_dim(values, col_start, width_local, 1)


def body(
    tokens,
    run_counts,
    seq_lengths,
    first_gain,
    in_weight,
    conv_weight,
    out_weight,
    second_gain,
    gate_weight,
    up_weight,
    down_weight,
    cotangent,
):
    cap_slots, width_local = tokens.shape
    col_start = lax.axis_index("col") * width_local
    row_index = lax.axis_index("row")
    run_ids = jnp.arange(run_counts.shape[0], dtype=jnp.int32)
    offsets = jnp.cumsum(run_counts) - run_counts
    own_count = jnp.sum(jnp.where(run_ids == row_index, run_counts, 0))
    own_offset = jnp.sum(jnp.where(run_ids == row_index, offsets, 0))
    slot_ids = jnp.arange(cap_slots, dtype=jnp.int32)
    position = own_offset + slot_ids
    is_live = slot_ids < own_count
    starts = jnp.cumsum(seq_lengths) - seq_lengths
    seq_start = jnp.max(jnp.where(starts[None, :] <= position[:, None], starts[None, :], 0), axis=1)
    live_mask = is_live.astype(jnp.float32)[:, None]
    valid_one = (is_live & (position - 1 >= seq_start)).astype(jnp.float32)[:, None]
    valid_two = (is_live & (position - 2 >= seq_start)).astype(jnp.float32)[:, None]
    in_full, out_full, gate_full, up_full, down_full = fetch_weights(
        in_weight, out_weight, gate_weight, up_weight, down_weight
    )
    tokens_full, gain_one, gain_two = (
        lax.all_gather(tokens, "col", axis=1, tiled=True),
        lax.all_gather(first_gain, "col", axis=0, tiled=True),
        lax.all_gather(second_gain, "col", axis=0, tiled=True),
    )
    x_full = tokens_full.astype(jnp.float32)
    gain_one = gain_one.astype(jnp.float32)
    gain_two = gain_two.astype(jnp.float32)
    scale_one = lax.rsqrt(jnp.mean(x_full * x_full, axis=1, keepdims=True) + epsilon)
    normed_one = x_full * scale_one
    h_one = (normed_one * gain_one).astype(jnp.bfloat16)
    proj = jnp.einsum("sd,dpe->spe", h_one, in_full, preferred_element_type=jnp.float32)
    b_part = proj[:, 0]
    c_part = proj[:, 1]
    x_part = proj[:, 2]
    prod = (b_part * x_part).astype(jnp.bfloat16)
    tail_rows = lax.dynamic_slice_in_dim(prod, own_count - 2, 2, 0)
    halo_rows = passed_along(tail_rows, "row", 1)
    prod_ext = jnp.concatenate([halo_rows, prod], axis=0).astype(jnp.float32)
    tap_zero = prod_ext[2:]
    tap_one = prod_ext[1 : cap_slots + 1]
    tap_two = prod_ext[:cap_slots]
    taps = conv_weight.astype(jnp.float32)
    conv = taps[0] * tap_zero + taps[1] * valid_one * tap_one + taps[2] * valid_two * tap_two
    mixed = (c_part * conv).astype(jnp.bfloat16)
    mixed_full = lax.all_gather(mixed, "col", axis=1, tiled=True)
    branch = jnp.dot(mixed_full, out_full, preferred_element_type=jnp.float32)
    resid = tokens.astype(jnp.float32) + branch
    resid_full = lax.all_gather(resid, "col", axis=1, tiled=True)
    scale_two = lax.rsqrt(jnp.mean(resid_full * resid_full, axis=1, keepdims=True) + epsilon)
    normed_two = resid_full * scale_two
    h_two = (normed_two * gain_two).astype(jnp.bfloat16)
    gate = jnp.dot(h_two, gate_full, preferred_element_type=jnp.float32)
    upval = jnp.dot(h_two, up_full, preferred_element_type=jnp.float32)
    sigma = jax.nn.sigmoid(gate)
    swish = gate * sigma
    hidden = (swish * upval).astype(jnp.bfloat16)
    hidden_full = lax.all_gather(hidden, "col", axis=1, tiled=True)
    ffn_out = jnp.dot(hidden_full, down_full, preferred_element_type=jnp.float32)
    block_out = (live_mask * (resid + ffn_out)).astype(jnp.bfloat16)
    res_grad = live_mask * cotangent.astype(jnp.float32)
    ffn_grad = res_grad.astype(jnp.bfloat16)
    down_grad = jnp.einsum("sf,se->fe", hidden_full, ffn_grad, preferred_element_type=jnp.float32)
    hid_part = jnp.einsum("se,fe->sf", ffn_grad, down_full, preferred_element_type=jnp.float32)
    hid_grad = lax.psum_scatter(hid_part, "col", scatter_dimension=1, tiled=True)
    gate_back = (hid_grad * upval * sigma * (1.0 + gate * (1.0 - sigma))).astype(jnp.bfloat16)
    up_back = (hid_grad * swish).astype(jnp.bfloat16)
    gate_grad = jnp.einsum("sd,sf->df", h_two, gate_back, preferred_element_type=jnp.float32)
    up_grad = jnp.einsum("sd,sf->df", h_two, up_back, preferred_element_type=jnp.float32)
    htwo_part = jnp.einsum("sf,df->sd", gate_back, gate_full, preferred_element_type=jnp.float32)
    htwo_part = htwo_part + jnp.einsum(
        "sf,df->sd", up_back, up_full, preferred_element_type=jnp.float32
    )
    htwo_grad = lax.psum(htwo_part, "col")
    ntwo_grad = htwo_grad * gain_two
    resid_back = scale_two * (
        ntwo_grad - normed_two * jnp.mean(ntwo_grad * normed_two, axis=1, keepdims=True)
    )
    gain_two_grad = jnp.sum(
        own_columns(htwo_grad, col_start, width_local)
        * own_columns(normed_two, col_start, width_local),
        axis=0,
    )
    resid_grad = res_grad + own_columns(resid_back, col_start, width_local)
    branch_grad = resid_grad.astype(jnp.bfloat16)
    out_grad = jnp.einsum("sd,se->de", mixed_full, branch_grad, preferred_element_type=jnp.float32)
    mixed_part = jnp.einsum("se,de->sd", branch_grad, out_full, preferred_element_type=jnp.float32)
    mixed_grad = lax.psum_scatter(mixed_part, "col", scatter_dimension=1, tiled=True)
    c_grad = mixed_grad * conv
    conv_grad = mixed_grad * c_part
    tap_grads = jnp.stack(
        [
            jnp.sum(conv_grad * tap_zero, axis=0),
            jnp.sum(conv_grad * valid_one * tap_one, axis=0),
            jnp.sum(conv_grad * valid_two * tap_two, axis=0),
        ],
        axis=0,
    )
    into_one = taps[1] * valid_one * conv_grad
    into_two = taps[2] * valid_two * conv_grad
    ext_grad = jnp.pad(into_one, ((1, 1), (0, 0))) + jnp.pad(into_two, ((0, 2), (0, 0)))
    prod_grad = taps[0] * conv_grad + ext_grad[2:]
    back_rows = passed_along(ext_grad[:2], "row", -1)
    tail_grad = lax.dynamic_slice_in_dim(prod_grad, own_count - 2, 2, 0) + back_rows
    prod_grad = lax.dynamic_update_slice_in_dim(prod_grad, tail_grad, own_count - 2, 0)
    proj_grad = jnp.stack([prod_grad * x_part, c_grad, prod_grad * b_part], axis=1).astype(
        jnp.bfloat16
    )
    in_grad = jnp.einsum("sd,spe->dpe", h_one, proj_grad, preferred_element_type=jnp.float32)
    hone_part = jnp.einsum("spe,dpe->sd", proj_grad, in_full, preferred_element_type=jnp.float32)
    hone_grad = lax.psum(hone_part.astype(jnp.bfloat16), "col").astype(jnp.float32)
    none_grad = hone_grad * gain_one
    x_back = scale_one * (
        none_grad - normed_one * jnp.mean(none_grad * normed_one, axis=1, keepdims=True)
    )
    gain_one_grad = jnp.sum(
        own_columns(hone_grad, col_start, width_local)
        * own_columns(normed_one, col_start, width_local),
        axis=0,
    )
    input_grad = resid_grad + own_columns(x_back, col_start, width_local)
    in_grad, out_grad, gate_grad, up_grad, down_grad = (
        lax.psum_scatter(
            in_grad.astype(jnp.bfloat16), "row", scatter_dimension=0, tiled=True
        ).astype(jnp.float32),
        lax.psum_scatter(
            out_grad.astype(jnp.bfloat16), "row", scatter_dimension=0, tiled=True
        ).astype(jnp.float32),
        lax.psum_scatter(
            gate_grad.astype(jnp.bfloat16), "row", scatter_dimension=0, tiled=True
        ).astype(jnp.float32),
        lax.psum_scatter(
            up_grad.astype(jnp.bfloat16), "row", scatter_dimension=0, tiled=True
        ).astype(jnp.float32),
        lax.psum_scatter(
            down_grad.astype(jnp.bfloat16), "row", scatter_dimension=0, tiled=True
        ).astype(jnp.float32),
    )
    gain_one_grad, gain_two_grad, tap_grads = lax.psum(
        (gain_one_grad, gain_two_grad, tap_grads), "row"
    )
    return (
        block_out,
        input_grad,
        gain_one_grad,
        in_grad,
        tap_grads,
        out_grad,
        gain_two_grad,
        gate_grad,
        up_grad,
        down_grad,
    )


def solution(mesh):
    return jax.shard_map(
        body,
        mesh=mesh,
        in_specs=(
            P("row", "col"),
            P(),
            P(),
            P("col"),
            P("row", None, "col"),
            P(None, "col"),
            P("row", "col"),
            P("col"),
            P("row", "col"),
            P("row", "col"),
            P("row", "col"),
            P("row", "col"),
        ),
        out_specs=(
            P("row", "col"),
            P("row", "col"),
            P("col"),
            P("row", None, "col"),
            P(None, "col"),
            P("row", "col"),
            P("col"),
            P("row", "col"),
            P("row", "col"),
            P("row", "col"),
        ),
        check_vma=False,
    )
```

profile of v0, /device:TPU:0, one launch (start us, length us, event | category | flops | bytes accessed | tf_op | source)
XLA Modules:
  0.0 852.5 jit_solution(16850956513375364178)
XLA Ops:
  9.4 11.1 %all-gather = bf16[4,1,256]{2,1,0:T(2,128)(2,1)S(1)} all-gather(bf16[1,1,256]{2,1,0:T(2,128)(2,1)S(1)} %reshape.130), channel_id=1, replica_groups=mesh['row'=32,'col'=4] {'col'}, dimensions={0}, use_global_device_ids=true | all-gather | bytes 2560 | tf_op jit(solution)/shard_map/all_gather | solution.py:64
  26.2 13.1 %all_gather.33 = bf16[256,1024]{1,0:T(8,128)(2,1)S(1)} all-gather(bf16[256,256]{1,0:T(8,128)(2,1)} %param.12), channel_id=1, replica_groups=mesh['row'=32,'col'=4] {'col'}, dimensions={1}, use_global_device_ids=true | all-gather | bytes 655360 | tf_op jit(solution)/shard_map/all_gather | solution.py:63
  41.7 14.3 %all-gather.9.cloned.1.call-done = bf16[1024,3,256]{2,0,1:T(8,128)(2,1)} async-done(((bf16[32,3,256]{2,0,1:T(8,128)(2,1)}), bf16[1024,3,256]{2,0,1:T(8,128)(2,1)}) %all-gather.9.cloned.1.call-update) | async-done | bytes 1572880 | tf_op jit(solution)/shard_map/all_gather | solution.py:17
  60.5 24.1 %all_gather.37 = bf16[1024,256]{1,0:T(8,128)(2,1)S(1)} all-gather(bf16[32,256]{1,0:T(8,128)(2,1)S(1)} %copy-done.22), channel_id=1, replica_groups=mesh['row'=32,'col'=4] {'row'}, dimensions={0}, use_global_device_ids=true | all-gather | bytes 540672 | tf_op jit(solution)/shard_map/all_gather | solution.py:18
  85.5 13.3 %all_gather.36 = bf16[256,1024]{1,0:T(8,128)(2,1)S(1)} all-gather(bf16[256,256]{1,0:T(8,128)(2,1)S(1)} %get-tuple-element.23), channel_id=1, replica_groups=mesh['row'=32,'col'=4] {'col'}, dimensions={1}, use_global_device_ids=true | all-gather | bytes 655360 | tf_op jit(solution)/shard_map/all_gather | solution.py:87
  101.8 4.6 fusion.26
  107.1 9.9 %all-gather.1 = bf16[4,1,256]{2,1,0:T(2,128)(2,1)S(1)} all-gather(bf16[1,1,256]{2,1,0:T(2,128)(2,1)S(1)} %reshape.132), channel_id=1, replica_groups=mesh['row'=32,'col'=4] {'col'}, dimensions={0}, use_global_device_ids=true | all-gather | bytes 2560 | tf_op jit(solution)/shard_map/all_gather | solution.py:65
  117.0 10.1 %all-gather.11.cloned.1.call-done = f32[256,1024]{1,0:T(8,128)} async-done(((f32[256,256]{1,0:T(8,128)}), f32[256,1024]{1,0:T(8,128)}) %all-gather.11.cloned.1.call-update) | async-done | bytes 1048592 | tf_op jit(solution)/shard_map/all_gather | solution.py:90
  130.4 43.3 %all-gather.15.cloned.1.call-done = bf16[1024,1152]{1,0:T(8,128)(2,1)} async-done(((bf16[32,1152]{1,0:T(8,128)(2,1)}), bf16[1024,1152]{1,0:T(8,128)(2,1)}) %all-gather.15.cloned.1.call-update) | async-done | bytes 2359312 | tf_op jit(solution)/shard_map/all_gather | solution.py:20
  173.7 3.6 fusion.36
  177.2 42.0 %all-gather.13.cloned.1.call-done = bf16[1024,1152]{1,0:T(8,128)(2,1)} async-done(((bf16[32,1152]{1,0:T(8,128)(2,1)}), bf16[1024,1152]{1,0:T(8,128)(2,1)}) %all-gather.13.cloned.1.call-update) | async-done | bytes 2359312 | tf_op jit(solution)/shard_map/all_gather | solution.py:19
  219.3 53.0 %reduce-scatter.8.cloned.1.call-done = f32[256,1152]{1,0:T(8,128)} async-done(((f32[256,4608]{1,0:T(8,128)}), f32[256,1152]{1,0:T(8,128)}) %reduce-scatter.8.cloned.1.call-update) | async-done | bytes 1179664 | tf_op jit(solution)/shard_map/reduce_scatter | solution.py:106
  272.3 4.5 multiply_convert_fusion
  280.9 45.8 %all-reduce.6.cloned.1.call-done = f32[256,1024]{1,0:T(8,128)} async-done(((f32[256,1024]{1,0:T(8,128)}), f32[256,1024]{1,0:T(8,128)}) %all-reduce.6.cloned.1.call-update) | async-done | bytes 1048592 | tf_op jit(solution)/shard_map/psum | solution.py:115
  339.8 16.6 %reduce-scatter.10.cloned.1.call-done = f32[256,256]{1,0:T(8,128)} async-done(((f32[256,1024]{1,0:T(8,128)}), f32[256,256]{1,0:T(8,128)}) %reduce-scatter.10.cloned.1.call-update) | async-done | bytes 262160 | tf_op jit(solution)/shard_map/reduce_scatter | solution.py:129
  366.1 24.8 %all-gather.17.cloned.1.call-done = bf16[256,4608]{1,0:T(8,128)(2,1)} async-done(((bf16[256,1152]{1,0:T(8,128)(2,1)}), bf16[256,4608]{1,0:T(8,128)(2,1)}) %all-gather.17.cloned.1.call-update) | async-done | bytes 2359312 | tf_op jit(solution)/shard_map/all_gather | solution.py:99
  391.0 3.9 convolution_convert_fusion
  394.9 76.2 %reduce-scatter.14.cloned.1.call-done = bf16[32,256]{1,0:T(8,128)(2,1)} async-done(((bf16[1024,256]{1,0:T(8,128)(2,1)}), bf16[32,256]{1,0:T(8,128)(2,1)}) %reduce-scatter.14.cloned.1.call-update) | async-done | bytes 16400 | tf_op jit(solution)/shard_map/reduce_scatter | solution.py:167
  472.4 80.7 %reduce-scatter.16.cloned.1.call-done = bf16[32,1152]{1,0:T(8,128)(2,1)} async-done(((bf16[1024,1152]{1,0:T(8,128)(2,1)}), bf16[32,1152]{1,0:T(8,128)(2,1)}) %reduce-scatter.16.cloned.1.call-update) | async-done | bytes 73744 | tf_op jit(solution)/shard_map/reduce_scatter | solution.py:170
  554.7 80.9 %reduce-scatter.18.cloned.1.call-done = bf16[32,1152]{1,0:T(8,128)(2,1)} async-done(((bf16[1024,1152]{1,0:T(8,128)(2,1)}), bf16[32,1152]{1,0:T(8,128)(2,1)}) %reduce-scatter.18.cloned.1.call-update) | async-done | bytes 73744 | tf_op jit(solution)/shard_map/reduce_scatter | solution.py:173
  640.3 40.4 %all-reduce.8.cloned.1.call-done = bf16[256,1024]{1,0:T(8,128)(2,1)} async-done(((bf16[256,1024]{1,0:T(8,128)(2,1)}), bf16[256,1024]{1,0:T(8,128)(2,1)}) %all-reduce.8.cloned.1.call-update) | async-done | bytes 524304 | tf_op jit(solution)/shard_map/psum | solution.py:152
  684.1 66.5 %all-reduce.2 = (f32[256]{0:T(256)}, f32[3,256]{1,0:T(4,128)}, f32[256]{0:T(256)}) all-reduce(f32[256]{0:T(256)S(1)} %get-tuple-element.30, f32[3,256]{1,0:T(4,128)S(1)} %pad_maximum_fusion.3, f32[256]{0:T(256)S(1)} %copy-done.32), channel_id=1, replica_groups=mesh['row'=32,'col'=4] {'row'}, use_global_device_ids=true, to_apply=%region_14.15 | all-reduce | flops 1280 | bytes 10240 | tf_op jit(solution)/shard_map/psum | solution.py:180
  750.5 12.0 %reduce-scatter.12.cloned.1.call-done = bf16[32,3,256]{2,0,1:T(8,128)(2,1)} async-done(((bf16[1024,3,256]{2,0,1:T(8,128)(2,1)}), bf16[32,3,256]{2,0,1:T(8,128)(2,1)}) %reduce-scatter.12.cloned.1.call-update) | async-done | bytes 49168 | tf_op jit(solution)/shard_map/reduce_scatter | solution.py:164
  764.0 80.5 %reduce-scatter.20.cloned.1.call-done = bf16[144,256]{1,0:T(8,128)(2,1)} async-done(((bf16[4608,256]{1,0:T(8,128)(2,1)}), bf16[144,256]{1,0:T(8,128)(2,1)}) %reduce-scatter.20.cloned.1.call-update) | async-done | bytes 73744 | tf_op jit(solution)/shard_map/reduce_scatter | solution.py:176
  (158 shorter events, 61.6 us)
Async XLA Ops:
  7.2 48.8 %all-gather.9.cloned.1.call-start = ((), (), s32[]{:S(2)}) async-start(), calls=%async_computation.7 | async-start | bytes 1622016 | tf_op jit(solution)/shard_map/all_gather | solution.py:17
  7.9 93.9 %all-gather.19.cloned.1.call-start = ((), (), s32[]{:S(2)}) async-start(), calls=%async_computation.12 | async-start | bytes 2433024 | tf_op jit(solution)/shard_map/all_gather | solution.py:21
  8.7 118.4 %all-gather.11.cloned.1.call-start = ((), (), s32[]{:S(2)}) async-start(), calls=%async_computation.8 | async-start | bytes 1310720 | tf_op jit(solution)/shard_map/all_gather | solution.py:90
  39.5 45.1 %copy-start.29 = (f32[256]{0:T(256)}, f32[256]{0:T(256)S(1)}, u32[]{:S(2)}) copy-start(f32[256]{0:T(256)S(1)} %add_rsqrt_fusion.1) | copy-start | bytes 3076
  40.8 44.6 %copy-start.16 = (f32[256]{0:T(256)}, f32[256]{0:T(256)S(1)}, u32[]{:S(2)}) copy-start(f32[256]{0:T(256)S(1)} %get-tuple-element.43) | copy-start | bytes 3076
  40.9 44.6 %copy-start.18 = (f32[256]{0:T(256)}, f32[256]{0:T(256)S(1)}, u32[]{:S(2)}) copy-start(f32[256]{0:T(256)S(1)} %get-tuple-element.44) | copy-start | bytes 3076
  41.7 43.8 %copy-start.25 = (f32[1,256]{1,0:T(1,128)}, f32[1,256]{1,0:T(1,128)S(1)}, u32[]{:S(2)}) copy-start(f32[1,256]{1,0:T(1,128)S(1)} %get-tuple-element.41) | copy-start | bytes 3076
  41.7 43.8 %copy-start.27 = (f32[1,256]{1,0:T(1,128)}, f32[1,256]{1,0:T(1,128)S(1)}, u32[]{:S(2)}) copy-start(f32[1,256]{1,0:T(1,128)S(1)} %get-tuple-element.42) | copy-start | bytes 3076
  58.2 26.4 %collective-permute-start = (bf16[2,256]{1,0:T(2,128)(2,1)S(1)}, bf16[2,256]{1,0:T(2,128)(2,1)S(1)}, u32[]{:S(2)}, u32[]{:S(2)}) collective-permute-start(bf16[2,256]{1,0:T(2,128)(2,1)S(1)} %constant_dynamic-slice_fusion), channel_id=1, source_target_pairs={{0,4},{4,8},{8,12},{12,16},{16,20},{20,24},{24,28},{28,32},{32,36}... | collective-permute-start | bytes 3080 | tf_op jit(solution)/shard_map/ppermute | solution.py:12
  99.9 73.8 %all-gather.15.cloned.1.call-start = ((), (), s32[]{:S(2)}) async-start(), calls=%async_computation.10 | async-start | bytes 2433024 | tf_op jit(solution)/shard_map/all_gather | solution.py:20
  100.5 118.8 %all-gather.13.cloned.1.call-start = ((), (), s32[]{:S(2)}) async-start(), calls=%async_computation.9 | async-start | bytes 2433024 | tf_op jit(solution)/shard_map/all_gather | solution.py:19
  101.1 171.2 %reduce-scatter.8.cloned.1.call-start = ((), (), s32[]{:S(2)}) async-start(), calls=%async_computation.13 | async-start | bytes 5898240 | tf_op jit(solution)/shard_map/reduce_scatter | solution.py:106
  106.5 220.2 %all-reduce.6.cloned.1.call-start = ((), (), s32[]{:S(2)}) async-start(), calls=%async_computation.14 | async-start | bytes 2097152 | tf_op jit(solution)/shard_map/psum | solution.py:115
  280.8 75.6 %reduce-scatter.10.cloned.1.call-start = ((), (), s32[]{:S(2)}) async-start(), calls=%async_computation.15 | async-start | bytes 1310720 | tf_op jit(solution)/shard_map/reduce_scatter | solution.py:129
  331.9 59.0 %all-gather.17.cloned.1.call-start = ((), (), s32[]{:S(2)}) async-start(), calls=%async_computation.11 | async-start | bytes 2949120 | tf_op jit(solution)/shard_map/all_gather | solution.py:99
  332.7 138.4 %reduce-scatter.14.cloned.1.call-start = ((), (), s32[]{:S(2)}) async-start(), calls=%async_computation.18 | async-start | bytes 540672 | tf_op jit(solution)/shard_map/reduce_scatter | solution.py:167
  334.9 218.3 %reduce-scatter.16.cloned.1.call-start = ((), (), s32[]{:S(2)}) async-start(), calls=%async_computation.19 | async-start | bytes 2433024 | tf_op jit(solution)/shard_map/reduce_scatter | solution.py:170
  337.3 298.3 %reduce-scatter.18.cloned.1.call-start = ((), (), s32[]{:S(2)}) async-start(), calls=%async_computation.20 | async-start | bytes 2433024 | tf_op jit(solution)/shard_map/reduce_scatter | solution.py:173
  339.8 340.9 %all-reduce.8.cloned.1.call-start = ((), (), s32[]{:S(2)}) async-start(), calls=%async_computation.16 | async-start | bytes 1048576 | tf_op jit(solution)/shard_map/psum | solution.py:152
  357.8 3.1 collective-permute-start.1
  363.9 398.6 %reduce-scatter.12.cloned.1.call-start = ((), (), s32[]{:S(2)}) async-start(), calls=%async_computation.17 | async-start | bytes 1622016 | tf_op jit(solution)/shard_map/reduce_scatter | solution.py:164
  366.1 478.4 %reduce-scatter.20.cloned.1.call-start = ((), (), s32[]{:S(2)}) async-start(), calls=%async_computation.21 | async-start | bytes 2433024 | tf_op jit(solution)/shard_map/reduce_scatter | solution.py:176
  394.9 242.2 %copy-start.1 = (bf16[256,4608]{1,0:T(8,128)(2,1)S(1)}, bf16[256,4608]{1,0:T(8,128)(2,1)}, u32[]{:S(2)}) copy-start(bf16[256,4608]{1,0:T(8,128)(2,1)} %all-gather.17.cloned.1.call-done) | copy-start | bytes 7077892
  394.9 242.2 %copy-start.14 = (f32[256,256]{1,0:T(8,128)S(1)}, f32[256,256]{1,0:T(8,128)}, u32[]{:S(2)}) copy-start(f32[256,256]{1,0:T(8,128)} %convolution_add_fusion.2) | copy-start | bytes 786436
  (27 other events, 455.3 us)
Sparse Core Ops, SparseCore 0:
  10.4 45.5 all-gather.8
  58.3 43.4 all-gather.18
  103.4 23.5 all-gather.10
  129.2 44.4 all-gather.14
  175.8 43.4 all-gather.12
  221.6 50.7 reduce-scatter.7
  280.9 45.6 all-reduce.5
  332.1 24.3 reduce-scatter.9
  358.1 32.8 all-gather.16
  394.3 76.7 reduce-scatter.13
  474.7 78.4 reduce-scatter.15
  557.0 78.5 reduce-scatter.17
  637.9 42.6 all-reduce.7
  684.0 78.4 reduce-scatter.11
  765.9 78.4 reduce-scatter.19
where the time goes:
time: 854 us; the launch traced here: 853 us
  waiting for transfers between devices  626 us (73%)
  blocking collectives  138 us (16%)
  matrix products  38.4 us (4%)
  other arithmetic  25 us (3%)
  between operations  15.7 us (2%)
    reduce_scatter x1, waiting for transfers between devices, body(): lax.psum_scatter(up_grad.astype(jnp.bfloat16), 'row', scatter_dimension=0...  80.9 us
    reduce_scatter x1, waiting for transfers between devices, body(): lax.psum_scatter(gate_grad.astype(jnp.bfloat16), 'row', scatter_dimension...  80.7 us
    reduce_scatter x1, waiting for transfers between devices, body(): lax.psum_scatter(down_grad.astype(jnp.bfloat16), 'row', scatter_dimension...  80.5 us
    reduce_scatter x1, waiting for transfers between devices, body(): lax.psum_scatter(out_grad.astype(jnp.bfloat16), 'row', scatter_dimension=...  76.2 us
    psum x1, blocking collectives, body(): lax.psum((gain_one_grad, gain_two_grad, tap_grads), 'row')  66.5 us
    reduce_scatter x1, waiting for transfers between devices, body(): lax.psum_scatter(hid_part, 'col', scatter_dimension=1, tiled=True)  53 us
    psum x1, waiting for transfers between devices, body(): htwo_grad = lax.psum(htwo_part, 'col')  45.8 us
    all_gather x1, waiting for transfers between devices, fetch_weights(): lax.all_gather(up_weight, 'row', axis=0, tiled=True)  43.3 us
  transfers between devices with their start and end apart: 17, of which 15 were waited for; matrix products, arithmetic and copies ran while one was open for 6% of the time, Pallas kernels for 0%

commit v1 on v0

v1 whole, which is shorter than its diff:
```python
import functools

import jax
import jax.numpy as jnp
from jax import lax
from jax.experimental import pallas as pl
from jax.experimental.pallas import tpu as pltpu
from jax.sharding import PartitionSpec as P

epsilon = 1e-05
MESH = pl.DeviceIdType.MESH
bf16, f32 = jnp.bfloat16, jnp.float32
SIDE = 4
RING = (1, 3, 2)
COPIES = 256


def dot(a, b):
    return lax.dot_general(a, b, (((1,), (0,)), ((), ())), preferred_element_type=f32)


def dot_nt(a, b):
    return lax.dot_general(a, b, (((1,), (1,)), ((), ())), preferred_element_type=f32)


def wrap(i):
    return lax.rem(i, SIDE)


def total(values):
    return functools.reduce(lambda a, b: a + b, values)


def kernel(
    tokens, run_counts, seq_lengths, first_gain, in_weight, conv_weight, out_weight, second_gain,
    gate_weight, up_weight, down_weight, cotangent,
    block_out, input_grad, first_gain_grad, in_grad, conv_grad, out_grad, second_gain_grad,
    gate_grad, up_grad, down_grad,
    in_b, out_b, gate_b, up_b, down_b,
    x_g, cot_g, r1_g, gh2_g, gains,
    o_s, o_r, gh2_s, gh2_r, ffo_s, ffo_r, gh1_s, gh1_r, dots,
    in_p, out_p, gate_p, up_p, down_p,
    in_1, out_1, gate_1, up_1, down_1,
    in_2a, in_2b, out_2a, out_2b, gate_2, up_2, down_2a, down_2b,
    in_3, out_3, gate_3, up_3, down_3,
    out_t, down_t,
    h1, h2, h1_t, h2_t, hid, hid_t, g_gate_ref, g_up, g_hid, g_proj, z_t, go,
    b_s, c_s, x_s, conv_s, tap1_s, tap2_s, r1_s, gr1_s, own_s, ffo_own, rs1_s,
    halo_s, halo_r, back_s, back_r, vec_a, vec_b, vec_x, vec_y,
    send, recv,
):
    row, z = lax.axis_index("row"), lax.axis_index("col")
    x, y, k = row // (2 * SIDE), wrap(row // 2), lax.rem(row, 2)
    slots, width = tokens.shape
    rows = 2 * SIDE * SIDE

    def at(x_to, y_to, k_to, z_to):
        return ((wrap(x_to) * SIDE + wrap(y_to)) * 2 + k_to, wrap(z_to))

    def x_peer(d):
        return at(x + d, y, k, z)

    def y_peer(d):
        return at(x, y + d, k, z)

    def z_peer(d):
        return (row, wrap(z + d))

    sibling = (row + 1 - 2 * k, z)
    mirror = at(z, y, k, x)
    next_row, last_row = (lax.rem(row + 1, rows), z), (lax.rem(row + rows - 1, rows), z)

    barrier = pltpu.get_barrier_semaphore()
    peers = [f(d) for f in (x_peer, y_peer, z_peer) for d in RING] + [next_row, last_row]
    for peer in peers:
        pl.semaphore_signal(barrier, inc=1, device_id=peer, device_id_type=MESH)

    @pl.when(x != z)
    def _():
        pl.semaphore_signal(barrier, inc=1, device_id=mirror, device_id_type=MESH)

    slot = lax.broadcasted_iota(jnp.int32, (slots, 1), 0)
    count = run_counts[row]
    offset = total([jnp.where(q < row, run_counts[q], 0) for q in range(rows)])
    position = offset + slot
    is_live = slot < count
    start, seq_start = 0, jnp.zeros((slots, 1), jnp.int32)
    for q in range(seq_lengths.shape[0]):
        seq_start = jnp.maximum(seq_start, jnp.where(position >= start, start, 0))
        start = start + seq_lengths[q]
    valid1 = is_live & (position - 1 >= seq_start)
    valid2 = is_live & (position - 2 >= seq_start)

    x_g[z] = tokens[...]
    cot_g[z] = jnp.where(is_live, cotangent[...].astype(f32), 0.0).astype(bf16)
    gains[z, 0:1, :] = first_gain[...].astype(f32)
    gains[z, 1:2, :] = second_gain[...].astype(f32)
    gains[z, 2:8, :] = jnp.zeros((6, width), f32)
    for p in range(3):
        in_b[x, y, k, :, p * width : (p + 1) * width] = in_weight[p]
    gate_b[x, y, k] = gate_weight[...]
    up_b[x, y, k] = up_weight[...]

    @pl.when(x != z)
    def _():
        pl.semaphore_wait(barrier, len(peers) + 1)

    @pl.when(x == z)
    def _():
        pl.semaphore_wait(barrier, len(peers))

    started = []

    def copy(src, dst, to):
        i = len(started)
        c = pltpu.make_async_remote_copy(
            src_ref=src,
            dst_ref=dst,
            send_sem=send.at[i],
            recv_sem=recv.at[i],
            device_id=to,
            device_id_type=MESH,
        )
        started.append(c)
        return c

    def launch(src, dst, to):
        c = copy(src, dst, to)
        c.start()
        return c

    def arrive(copies):
        for c in copies:
            c.wait_recv()

    def gather_z(buf):
        return [launch(buf.at[z], buf.at[z], z_peer(d)) for d in RING]

    class Gather:
        def __init__(self, buf, first, cols=None):
            self.buf, self.first = buf, first
            self.cols = slice(None) if cols is None else pl.ds(*cols)

        def ring_one(self):
            own = self.buf.at[x, y, k, :, self.cols]
            peer = x_peer if self.first == "x" else y_peer
            self.pending = [launch(own, own, peer(d)) for d in RING]

        def ring_two(self):
            arrive(self.pending)
            if self.first == "x":
                part, peer = self.buf.at[:, y, k, :, self.cols], y_peer
            else:
                part, peer = self.buf.at[x, :, k, :, self.cols], x_peer
            self.pending = [launch(part, part, peer(d)) for d in RING]

        def core(self):
            arrive(self.pending)
            part = self.buf.at[:, :, k, :, self.cols]
            self.pending = [launch(part, part, sibling)]

        def done(self):
            arrive(self.pending)

    class Scatter:
        def __init__(self, partial, one, parts, three):
            self.partial, self.one, self.parts, self.three = partial, one, parts, three

        def core(self):
            self.pending = [launch(self.partial.at[:, :, 1 - k], self.one, sibling)]

        def ring_one(self):
            arrive(self.pending)
            one, partial = self.one, self.partial

            @pl.loop(0, SIDE * SIDE)
            def _(i):
                a, b = i // SIDE, wrap(i)
                one[a, b] = (partial[a, b, k].astype(f32) + one[a, b].astype(f32)).astype(bf16)

            self.pending = []
            for two, first, cols in self.parts:
                cs = pl.ds(*cols)
                sent = []
                for d in RING:
                    if first == "x":
                        part, peer, me = one.at[wrap(x + d), :, :, cs], x_peer(d), x
                    else:
                        part, peer, me = one.at[:, wrap(y + d), :, cs], y_peer(d), y
                    sent.append(launch(part, two.at[me], peer))
                self.pending.append(sent)
                if first == "x":
                    two[x] = one[x, :, :, cs]
                else:
                    two[y] = one[:, y, :, cs]

        def ring_two(self):
            later = []
            for (two, first, cols), sent in zip(self.parts, self.pending):
                arrive(sent)
                me = x if first == "x" else y

                @pl.loop(0, SIDE)
                def _(j):
                    two[me, j] = total([two[s, j].astype(f32) for s in range(SIDE)]).astype(bf16)

                cs = pl.ds(*cols)
                for d in RING:
                    if first == "x":
                        part, peer, to = two.at[x, wrap(y + d)], y_peer(d), y
                    else:
                        part, peer, to = two.at[y, wrap(x + d)], x_peer(d), x
                    later.append(launch(part, self.three.at[to, :, cs], peer))
                if first == "x":
                    self.three[y, :, cs] = two[x, y]
                else:
                    self.three[x, :, cs] = two[y, x]
            self.pending = later

        def done(self):
            arrive(self.pending)
            return total([self.three[s].astype(f32) for s in range(SIDE)])

    got_x = gather_z(x_g) + gather_z(gains)
    in_half = in_b.shape[-1] // 2
    g_in = [Gather(in_b, "x", (0, in_half)), Gather(in_b, "y", (in_half, in_half))]
    for g in g_in:
        g.ring_one()
    swap_out = copy(out_weight, out_b.at[z, y, k], mirror)
    swap_down = copy(down_weight, down_b.at[z, y, k], mirror)

    @pl.when(x != z)
    def _():
        swap_out.start()
        swap_down.start()

    @pl.when(x == z)
    def _():
        out_b[x, y, k] = out_weight[...]
        down_b[x, y, k] = down_weight[...]

    for g in g_in:
        g.ring_two()

    @pl.when(x != z)
    def _():
        swap_out.wait_recv()
        swap_down.wait_recv()

    half = width // 2
    g_out = [Gather(out_b, "x", (0, half)), Gather(out_b, "y", (half, half))]
    g_down = [Gather(down_b, "x", (0, half)), Gather(down_b, "y", (half, half))]
    w_gate, w_up = Gather(gate_b, "x"), Gather(up_b, "y")
    for g in g_out:
        g.ring_one()
    w_gate.ring_one()
    w_up.ring_one()
    got_cot = gather_z(cot_g)

    arrive(got_x)
    features = SIDE * width
    squares = total([jnp.sum(jnp.square(x_g[i].astype(f32)), axis=1, keepdims=True) for i in range(SIDE)])
    rs1_s[...] = lax.rsqrt(squares / features + epsilon)
    for i in range(SIDE):
        h = ((x_g[i].astype(f32) * rs1_s[...]) * gains[i, 0:1, :]).astype(bf16)
        h1[:, i * width : (i + 1) * width] = h
    for g in g_in:
        g.core()
    for g in g_out:
        g.ring_two()
    w_gate.ring_two()
    w_up.ring_two()
    for g in g_down:
        g.ring_one()
    for i in range(SIDE):
        h1_t[i] = h1[:, i * width : (i + 1) * width].T

    for g in g_in:
        g.done()
    for p, ref in enumerate((b_s, c_s, x_s)):
        w = in_b[:, :, :, :, p * width : (p + 1) * width].reshape(features, width)
        ref[...] = dot(h1[...], w)
    u = (b_s[...] * x_s[...]).astype(bf16).astype(f32)
    halo_s[...] = jnp.zeros(halo_s.shape, f32)
    halo_s[0:1, :] = jnp.sum(jnp.where(slot == count - 2, u, 0.0), axis=0, keepdims=True)
    halo_s[1:2, :] = jnp.sum(jnp.where(slot == count - 1, u, 0.0), axis=0, keepdims=True)
    got_halo = launch(halo_s, halo_r, next_row)
    for g in g_out:
        g.core()
    taps = conv_weight[...].astype(f32)
    tap1 = pltpu.roll(u, 1, 0)
    tap2 = pltpu.roll(u, 2, 0)
    for g in g_out:
        g.done()
    got_halo.wait_recv()
    halo = halo_r[...]
    tap1 = jnp.where(valid1, jnp.where(slot == 0, halo[1:2], tap1), 0.0)
    tap2 = jnp.where(valid2, jnp.where(slot == 0, halo[0:1], jnp.where(slot == 1, halo[1:2], tap2)), 0.0)
    tap1_s[...] = tap1
    tap2_s[...] = tap2
    conv = taps[0:1] * u + taps[1:2] * tap1 + taps[2:3] * tap2
    conv_s[...] = conv
    mixed = (c_s[...] * conv).astype(bf16)
    z_t[...] = mixed.T

    got_o = []
    for d in RING:
        i = wrap(z + d)
        o_s[i] = dot(mixed, out_b[i].reshape(width, width)).astype(bf16)
        got_o.append(launch(o_s.at[i], o_r.at[z], z_peer(d)))
    r1_s[...] = tokens[...].astype(f32) + dot(mixed, out_b[z].reshape(width, width))
    for g in g_down:
        g.ring_two()
    arrive(got_o)
    r1 = r1_s[...] + total([o_r[wrap(z + d)].astype(f32) for d in RING])
    r1_s[...] = r1
    r1_g[z] = r1.astype(bf16)
    got_r1 = gather_z(r1_g)

    arrive(got_cot)
    w_gate.core()
    w_up.core()
    for g in g_down:
        g.core()
    for g in g_down:
        g.done()
    units = hid.shape[1]
    g_hid[...] = total([dot_nt(cot_g[i], down_b[i].reshape(units, width)) for i in range(SIDE)])

    arrive(got_r1)
    squares = total([jnp.sum(jnp.square(r1_g[i].astype(f32)), axis=1, keepdims=True) for i in range(SIDE)])
    rs2 = lax.rsqrt(squares / features + epsilon)
    for i in range(SIDE):
        h = ((r1_g[i].astype(f32) * rs2) * gains[i, 1:2, :]).astype(bf16)
        h2[:, i * width : (i + 1) * width] = h

    w_gate.done()
    w_up.done()
    tile = units // 3
    for n in range(3):
        cs = slice(n * tile, (n + 1) * tile)
        gate = dot(h2[...], gate_b[:, :, :, :, cs].reshape(features, tile))
        up = dot(h2[...], up_b[:, :, :, :, cs].reshape(features, tile))
        sigma = jax.nn.sigmoid(gate)
        swish = gate * sigma
        grad = g_hid[:, cs]
        hid[:, cs] = (swish * up).astype(bf16)
        g_gate_n = grad * up * sigma * (1.0 + gate * (1.0 - sigma))
        g_gate_ref[:, cs] = g_gate_n.astype(bf16)
        g_up[:, cs] = (grad * swish).astype(bf16)

    def h2_part(i):
        return dot_nt(g_gate_ref[...], gate_b[i].reshape(width, units)) + dot_nt(
            g_up[...], up_b[i].reshape(width, units)
        )

    got_gh2 = []
    for d in RING:
        i = wrap(z + d)
        gh2_s[i] = h2_part(i).astype(bf16)
        got_gh2.append(launch(gh2_s.at[i], gh2_r.at[z], z_peer(d)))
    own_s[...] = h2_part(z)
    hid_t[...] = hid[...].T

    @pl.loop(0, SIDE)
    def _(i):
        down_p[i] = dot(hid_t[...], cot_g[i]).astype(bf16).reshape(down_p.shape[1:])

    s_down = Scatter(down_p, down_1, [(down_2a, "x", (0, half)), (down_2b, "y", (half, half))], down_3)
    s_down.core()
    for i in range(SIDE):
        h2_t[i] = h2[:, i * width : (i + 1) * width].T

    @pl.loop(0, SIDE)
    def _(i):
        gate_p[i] = dot(h2_t[i], g_gate_ref[...]).astype(bf16).reshape(gate_p.shape[1:])

    s_gate = Scatter(gate_p, gate_1, [(gate_2, "x", (0, units))], gate_3)
    s_gate.core()
    arrive(got_gh2)
    gh2_g[z] = (own_s[...] + total([gh2_r[wrap(z + d)].astype(f32) for d in RING])).astype(bf16)
    got_gh2 = gather_z(gh2_g)
    s_down.ring_one()

    @pl.loop(0, SIDE)
    def _(i):
        up_p[i] = dot(h2_t[i], g_up[...]).astype(bf16).reshape(up_p.shape[1:])

    s_up = Scatter(up_p, up_1, [(up_2, "y", (0, units))], up_3)
    s_up.core()
    s_gate.ring_one()
    s_up.ring_one()

    arrive(got_gh2)
    mean2 = total(
        [
            jnp.sum(gh2_g[i].astype(f32) * gains[i, 1:2, :] * (r1_g[i].astype(f32) * rs2), axis=1, keepdims=True)
            for i in range(SIDE)
        ]
    ) / features

    def r1_grad(i):
        n2 = r1_g[i].astype(f32) * rs2
        return cot_g[i].astype(f32) + rs2 * (gh2_g[i].astype(f32) * gains[i, 1:2, :] - n2 * mean2)

    for i in range(SIDE):
        go[i] = r1_grad(i).astype(bf16)
    gr1_s[...] = r1_grad(z)
    vec_a[...] = jnp.zeros(vec_a.shape, f32)
    vec_a[0:1, :] = jnp.sum(gh2_g[z].astype(f32) * (r1_g[z].astype(f32) * rs2), axis=0, keepdims=True)

    g_z = total([dot_nt(go[i], out_b[i].reshape(width, width)) for i in range(SIDE)])
    g_c = g_z * conv_s[...]
    g_v = g_z * c_s[...]
    u = (b_s[...] * x_s[...]).astype(bf16).astype(f32)
    into1 = jnp.where(valid1, taps[1:2] * g_v, 0.0)
    into2 = jnp.where(valid2, taps[2:3] * g_v, 0.0)
    back_s[...] = jnp.zeros(back_s.shape, f32)
    back_s[0:1, :] = into2[0:1, :]
    back_s[1:2, :] = into1[0:1, :] + into2[1:2, :]
    got_back = launch(back_s, back_r, last_row)
    vec_a[1:2, :] = jnp.sum(g_v * u, axis=0, keepdims=True)
    vec_a[2:3, :] = jnp.sum(g_v * tap1_s[...], axis=0, keepdims=True)
    vec_a[3:4, :] = jnp.sum(g_v * tap2_s[...], axis=0, keepdims=True)
    g_u = taps[0:1] * g_v
    g_u = g_u + jnp.where(slot < slots - 1, pltpu.roll(into1, slots - 1, 0), 0.0)
    g_u = g_u + jnp.where(slot < slots - 2, pltpu.roll(into2, slots - 2, 0), 0.0)
    got_back.wait_recv()
    back = back_r[...]
    g_u = g_u + jnp.where(slot == count - 2, back[0:1], 0.0) + jnp.where(slot == count - 1, back[1:2], 0.0)
    g_proj[:, 0:width] = (g_u * x_s[...]).astype(bf16)
    g_proj[:, width : 2 * width] = g_c.astype(bf16)
    g_proj[:, 2 * width : 3 * width] = (g_u * b_s[...]).astype(bf16)

    for i in range(SIDE):
        in_p[i] = dot(h1_t[i], g_proj[...]).astype(bf16).reshape(in_p.shape[1:])
    s_in = Scatter(in_p, in_1, [(in_2a, "x", (0, in_half)), (in_2b, "y", (in_half, in_half))], in_3)
    s_in.core()

    ones = jnp.ones((8, width), bf16)

    def h1_part(i):
        part = dot_nt(g_proj[...], in_b[i].reshape(width, 3 * width))
        n1 = x_g[i].astype(f32) * rs1_s[...]
        return part, dot_nt(ones, (part * gains[i, 0:1, :] * n1).astype(bf16))

    got_gh1, along = [], []
    for d in RING:
        i = wrap(z + d)
        part, one = h1_part(i)
        along.append(one)
        gh1_s[i] = part.astype(bf16)
        got_gh1.append(launch(gh1_s.at[i], gh1_r.at[z], z_peer(d)))
    part, one = h1_part(z)
    own_s[...] = part
    dots[z] = total(along) + one
    got_gh1 += gather_z(dots)
    s_in.ring_one()

    for i in range(SIDE):
        out_p[i] = dot(z_t[...], go[i]).astype(bf16).reshape(out_p.shape[1:])
    s_out = Scatter(out_p, out_1, [(out_2a, "x", (0, half)), (out_2b, "y", (half, half))], out_3)
    s_out.core()

    got_ffo = []
    for d in RING:
        i = wrap(z + d)
        ffo_s[i] = dot(hid[...], down_b[i].reshape(units, width)).astype(bf16)
        got_ffo.append(launch(ffo_s.at[i], ffo_r.at[z], z_peer(d)))
    ffo_own[...] = r1_s[...] + dot(hid[...], down_b[z].reshape(units, width))

    s_down.ring_two()
    s_out.ring_one()
    s_gate.ring_two()
    s_up.ring_two()

    arrive(got_gh1)
    gh1 = own_s[...] + total([gh1_r[wrap(z + d)].astype(f32) for d in RING])
    mean1 = total([dots[i] for i in range(SIDE)]).T[:, 0:1] / features
    n1 = tokens[...].astype(f32) * rs1_s[...]
    input_grad[...] = gr1_s[...] + rs1_s[...] * (gh1 * gains[z, 0:1, :] - n1 * mean1)
    vec_a[4:5, :] = jnp.sum(gh1 * n1, axis=0, keepdims=True)
    got_vec = launch(vec_a, vec_b, sibling)

    down_t[...] = s_down.done()
    back_down = copy(down_t, down_grad, mirror)

    @pl.when(x != z)
    def _():
        back_down.start()

    @pl.when(x == z)
    def _():
        down_grad[...] = down_t[...]

    s_in.ring_two()
    s_out.ring_two()
    got_vec.wait_recv()
    vec_x[x] = vec_a[...] + vec_b[...]
    got_vec = [launch(vec_x.at[x], vec_x.at[x], x_peer(d)) for d in RING]
    gate_grad[...] = s_gate.done()
    up_grad[...] = s_up.done()
    arrive(got_vec)
    vec_y[y] = total([vec_x[s] for s in range(SIDE)])
    got_vec = [launch(vec_y.at[y], vec_y.at[y], y_peer(d)) for d in RING]
    out_t[...] = s_out.done()
    back_out = copy(out_t, out_grad, mirror)

    @pl.when(x != z)
    def _():
        back_out.start()

    @pl.when(x == z)
    def _():
        out_grad[...] = out_t[...]

    arrive(got_ffo)
    ffo = ffo_own[...] + total([ffo_r[wrap(z + d)].astype(f32) for d in RING])
    block_out[...] = jnp.where(is_live, ffo, 0.0).astype(bf16)
    in_sum = s_in.done()
    for p in range(3):
        in_grad[p] = in_sum[:, p * width : (p + 1) * width]
    arrive(got_vec)
    vec = total([vec_y[s] for s in range(SIDE)])
    second_gain_grad[...] = vec[0:1]
    conv_grad[...] = vec[1:4]
    first_gain_grad[...] = vec[4:5]

    mirrored = (swap_out, swap_down, back_down, back_out)

    @pl.when(x != z)
    def _():
        arrive((back_down, back_out))
        for c in mirrored:
            c.wait_send()

    for c in started:
        if not any(c is m for m in mirrored):
            c.wait_send()


def body(
    tokens,
    run_counts,
    seq_lengths,
    first_gain,
    in_weight,
    conv_weight,
    out_weight,
    second_gain,
    gate_weight,
    up_weight,
    down_weight,
    cotangent,
):
    slots, width = tokens.shape
    wide = in_weight.shape[0]
    units, deep = gate_weight.shape[1], down_weight.shape[0]
    three = 3 * width
    features = SIDE * width

    def vm(*shape, dtype=bf16):
        return pltpu.VMEM(shape, dtype)

    gathered = [
        vm(SIDE, SIDE, 2, r, w)
        for r, w in ((wide, three), (wide, width), (wide, units), (wide, units), (deep, width))
    ]
    by_col = [vm(SIDE, slots, width) for _ in range(4)] + [vm(SIDE, 8, width, dtype=f32)]
    summed = [vm(SIDE, slots, width) for _ in range(8)] + [vm(SIDE, 8, slots, dtype=f32)]
    ones = [
        vm(SIDE, SIDE, r, w)
        for r, w in ((wide, three), (wide, width), (wide, units), (wide, units), (deep, width))
    ]
    twos = [
        vm(SIDE, SIDE, r, w)
        for r, w in (
            (wide, three // 2), (wide, three // 2), (wide, width // 2), (wide, width // 2),
            (wide, units), (wide, units), (deep, width // 2), (deep, width // 2),
        )
    ]
    threes = [
        vm(SIDE, r, w)
        for r, w in ((wide, three), (wide, width), (wide, units), (wide, units), (deep, width))
    ]
    turned = [vm(wide, width, dtype=f32), vm(deep, width, dtype=f32)]
    own = [
        vm(slots, features), vm(slots, features), vm(SIDE, width, slots), vm(SIDE, width, slots),
        vm(slots, units), vm(units, slots), vm(slots, units), vm(slots, units),
        vm(slots, units, dtype=f32), vm(slots, three), vm(width, slots), vm(SIDE, slots, width),
    ]
    own += [vm(slots, width, dtype=f32) for _ in range(10)] + [vm(slots, 1, dtype=f32)]
    small = [vm(8, width, dtype=f32) for _ in range(6)] + [vm(SIDE, 8, width, dtype=f32) for _ in range(2)]
    scratch = gathered + by_col + summed + gathered + ones + twos + threes + turned + own + small
    scratch += [pltpu.SemaphoreType.DMA((COPIES,)), pltpu.SemaphoreType.DMA((COPIES,))]

    vmem, smem = pl.BlockSpec(memory_space=pltpu.VMEM), pl.BlockSpec(memory_space=pltpu.SMEM)

    def out(*shape, dtype=f32):
        return jax.ShapeDtypeStruct(shape, dtype)

    (block_out, input_grad, first_grad, in_grad, conv_grad, out_grad, second_grad, gate_grad, up_grad, down_grad) = (
        pl.pallas_call(
            kernel,
            out_shape=(
                out(slots, width, dtype=bf16), out(slots, width), out(1, width), out(3, wide, width), out(3, width),
                out(wide, width), out(1, width), out(wide, units), out(wide, units), out(deep, width),
            ),
            in_specs=[vmem, smem, smem] + [vmem] * 9,
            out_specs=(vmem,) * 10,
            scratch_shapes=scratch,
            compiler_params=pltpu.CompilerParams(
                collective_id=0, has_side_effects=True, vmem_limit_bytes=60 * 2**20
            ),
            name="block",
        )(
            tokens, run_counts, seq_lengths, first_gain.reshape(1, width), in_weight.transpose(1, 0, 2), conv_weight,
            out_weight, second_gain.reshape(1, width), gate_weight, up_weight, down_weight, cotangent,
        )
    )
    return (
        block_out,
        input_grad,
        first_grad.reshape(width),
        in_grad.transpose(1, 0, 2),
        conv_grad,
        out_grad,
        second_grad.reshape(width),
        gate_grad,
        up_grad,
        down_grad,
    )


def solution(mesh):
    return jax.shard_map(
        body,
        mesh=mesh,
        in_specs=(
            P("row", "col"),
            P(),
            P(),
            P("col"),
            P("row", None, "col"),
            P(None, "col"),
            P("row", "col"),
            P("col"),
            P("row", "col"),
            P("row", "col"),
            P("row", "col"),
            P("row", "col"),
        ),
        out_specs=(
            P("row", "col"),
            P("row", "col"),
            P("col"),
            P("row", None, "col"),
            P(None, "col"),
            P("row", "col"),
            P("col"),
            P("row", "col"),
            P("row", "col"),
            P("row", "col"),
        ),
        check_vma=False,
    )
```

time: 854 us -> 128 us (0.15)
  waiting for transfers between devices: 626 us -> 0 us
  blocking collectives: 138 us -> 0 us
  Pallas kernels: 0 us -> 118 us
  matrix products: 38.4 us -> 0 us
  other arithmetic: 25 us -> 0 us
  between operations: 15.7 us -> 0.68 us
    reduce_scatter x7 -> x0, waiting for transfers between devices: 400 us -> none  [the longest x1 80.9 us: body(): lax.psum_scatter(up_grad.astype(jnp.bfloat16), 'row', scatter_dimension=0...]
    all_gather x6 -> x0, waiting for transfers between devices: 135 us -> none  [the longest x1 43.3 us: fetch_weights(): lax.all_gather(up_weight, 'row', axis=0, tiled=True)]
    pallas_call x0 -> x1, Pallas kernels: none -> 118 us  [body(): pl.pallas_call(kernel, out_shape=(out(slots, width, dtype=bf16), out(slot...]
    psum x2 -> x0, waiting for transfers between devices: 86.2 us -> none  [the longest x1 45.8 us: body(): htwo_grad = lax.psum(htwo_part, 'col')]
    all_gather x5 -> x0, blocking collectives: 71.5 us -> none  [the longest x1 24.1 us: fetch_weights(): lax.all_gather(out_weight, 'row', axis=0, tiled=True)]
    psum x1 -> x0, blocking collectives: 66.5 us -> none  [body(): lax.psum((gain_one_grad, gain_two_grad, tap_grads), 'row')]
    dot_general x15 -> x0, matrix products: 38.4 us -> none  [the longest x1 4.61 us: body(): jnp.einsum('se,fe->sf', ffn_grad, down_full, preferred_element_type=jnp.f...]
    convert_element_type x14 -> x0, other arithmetic: 12.9 us -> none  [the longest x5 7.44 us: body(): in_grad, out_grad, gate_grad, up_grad, down_grad = (lax.psum_scatter(in_g...]
  transfers between devices with their start and end apart: 17 -> 0, of which waited for: 15 -> 0; matrix products, arithmetic and copies ran while one was open for 6% -> 0% of each run, Pallas kernels for 0% -> 0%
where the time goes in v1:
time: 128 us
  Pallas kernels  118 us (92%)
  local copies, waits for them, and re-layouts  9.84 us (8%)
    pallas_call x1, Pallas kernels, body(): pl.pallas_call(kernel, out_shape=(out(slots, width, dtype=bf16), out(slot...  118 us
    unnamed x32, local copies, waits for them, and re-layouts  8.71 us

profile of v1, /device:TPU:0, one launch (start us, length us, event | category | flops | bytes accessed | tf_op | source)
XLA Modules:
  0.0 128.0 jit_solution(445487040175843755)
XLA Ops:
  0.6 0.0 copy-start.9
  0.7 0.6 copy-done.9
  1.3 0.6 reshape.32.first_gain
  1.9 0.1 copy-done.10
  2.0 0.6 reshape.33.second_gain
  2.5 117.5 %block.1 = (bf16[256,256]{1,0:T(8,128)(2,1)}, f32[256,256]{1,0:T(8,128)}, f32[1,256]{1,0:T(1,128)}, f32[3,32,256]{2,1,0:T(8,128)}, f32[3,256]{1,0:T(4,128)}, /*i...) custom-call(bf16[256,256]{1,0:T(8,128)(2,1)} %tokens.1, ...), custom_call_target="tpu_custom_call" | custom-call | tf_op jit(solution)/shard_map/block/pallas_call | solution.py:603
  120.0 0.0 copy-start
  120.0 1.6 %copy.32 = bf16[256,256]{1,0:T(8,128)(2,1)} copy(bf16[256,256]{1,0:T(8,128)(2,1)} %get-tuple-element.40) | data formatting | bytes 262144
  121.7 0.0 copy-done
  121.7 0.7 copy.33
  122.4 0.0 copy-done.8
  122.4 0.6 copy.34
  122.9 0.0 copy-done.4
  122.9 0.6 copy.35
  123.6 0.0 copy-done.6
  123.6 0.6 copy.36
  124.2 0.6 copy.37
  124.8 0.0 copy-done.7
  124.9 0.6 copy.38
  125.4 0.7 copy.39
  126.1 0.3 copy-done.2
  126.4 0.7 copy.40
  127.1 0.3 copy-done.1
  127.4 0.7 copy.41
  (11 shorter events, 0.0 us)
Async XLA Ops:
  0.6 0.7 copy-start.9
  1.3 0.7 copy-start.10
  120.0 1.6 %copy-start = (f32[256,256]{1,0:T(8,128)S(1)}, f32[256,256]{1,0:T(8,128)}, u32[]{:S(2)}) copy-start(f32[256,256]{1,0:T(8,128)} %get-tuple-element.41) | copy-start | bytes 786436
  121.7 0.7 copy-start.8
  121.7 1.3 copy-start.4
  122.4 3.1 %copy-start.3 = (f32[32,1152]{1,0:T(8,128)S(1)}, f32[32,1152]{1,0:T(8,128)}, u32[]{:S(2)}) copy-start(f32[32,1152]{1,0:T(8,128)} %get-tuple-element.47) | copy-start | bytes 442372
  122.9 0.7 copy-start.6
  122.9 1.3 copy-start.5
  124.2 0.7 copy-start.7
  125.4 1.0 copy-start.2
  126.4 1.0 copy-start.1

commit v2 on v1

--- a/solution.py
+++ b/solution.py
@@ -41,13 +41,13 @@
     o_s, o_r, gh2_s, gh2_r, ffo_s, ffo_r, gh1_s, gh1_r, dots,
     in_p, out_p, gate_p, up_p, down_p,
     in_1, out_1, gate_1, up_1, down_1,
-    in_2a, in_2b, out_2a, out_2b, gate_2, up_2, down_2a, down_2b,
+    in_2a, in_2b, out_2, gate_2, up_2, down_2a, down_2b,
     in_3, out_3, gate_3, up_3, down_3,
-    out_t, down_t,
+    out_t, down_t, out_i, down_i,
     h1, h2, h1_t, h2_t, hid, hid_t, g_gate_ref, g_up, g_hid, g_proj, z_t, go,
     b_s, c_s, x_s, conv_s, tap1_s, tap2_s, r1_s, gr1_s, own_s, ffo_own, rs1_s,
-    halo_s, halo_r, back_s, back_r, vec_a, vec_b, vec_x, vec_y,
-    send, recv,
+    tail_s, back_s, back_r, vec_a, vec_b, vec_x, vec_y, tail_g,
+    send, recv, brought,
 ):
     row, z = lax.axis_index("row"), lax.axis_index("col")
     x, y, k = row // (2 * SIDE), wrap(row // 2), lax.rem(row, 2)
@@ -70,6 +70,21 @@
     mirror = at(z, y, k, x)
     next_row, last_row = (lax.rem(row + 1, rows), z), (lax.rem(row + rows - 1, rows), z)
 
+    local = []
+
+    def bring(src, dst):
+        c = pltpu.make_async_copy(src, dst, brought.at[len(local)])
+        local.append(c)
+        c.start()
+
+    for p in range(3):
+        bring(in_weight.at[p], in_b.at[x, y, k, :, p * width : (p + 1) * width])
+    bring(tokens, x_g.at[z])
+    bring(gate_weight, gate_b.at[x, y, k])
+    bring(up_weight, up_b.at[x, y, k])
+    bring(cotangent, cot_g.at[z])
+    bring(out_weight, out_i)
+    bring(down_weight, down_i)
     barrier = pltpu.get_barrier_semaphore()
     peers = [f(d) for f in (x_peer, y_peer, z_peer) for d in RING] + [next_row, last_row]
     for peer in peers:
@@ -79,27 +94,11 @@
     def _():
         pl.semaphore_signal(barrier, inc=1, device_id=mirror, device_id_type=MESH)
 
-    slot = lax.broadcasted_iota(jnp.int32, (slots, 1), 0)
-    count = run_counts[row]
-    offset = total([jnp.where(q < row, run_counts[q], 0) for q in range(rows)])
-    position = offset + slot
-    is_live = slot < count
-    start, seq_start = 0, jnp.zeros((slots, 1), jnp.int32)
-    for q in range(seq_lengths.shape[0]):
-        seq_start = jnp.maximum(seq_start, jnp.where(position >= start, start, 0))
-        start = start + seq_lengths[q]
-    valid1 = is_live & (position - 1 >= seq_start)
-    valid2 = is_live & (position - 2 >= seq_start)
-
-    x_g[z] = tokens[...]
-    cot_g[z] = jnp.where(is_live, cotangent[...].astype(f32), 0.0).astype(bf16)
-    gains[z, 0:1, :] = first_gain[...].astype(f32)
-    gains[z, 1:2, :] = second_gain[...].astype(f32)
+    gains[z, 0:1, :] = first_gain[...].astype(f32).reshape(1, width)
+    gains[z, 1:2, :] = second_gain[...].astype(f32).reshape(1, width)
     gains[z, 2:8, :] = jnp.zeros((6, width), f32)
-    for p in range(3):
-        in_b[x, y, k, :, p * width : (p + 1) * width] = in_weight[p]
-    gate_b[x, y, k] = gate_weight[...]
-    up_b[x, y, k] = up_weight[...]
+    for c in local:
+        c.wait()
 
     @pl.when(x != z)
     def _():
@@ -221,13 +220,39 @@
             arrive(self.pending)
             return total([self.three[s].astype(f32) for s in range(SIDE)])
 
-    got_x = gather_z(x_g) + gather_z(gains)
     in_half = in_b.shape[-1] // 2
+    half = width // 2
     g_in = [Gather(in_b, "x", (0, in_half)), Gather(in_b, "y", (in_half, in_half))]
+    g_out = Gather(out_b, "x")
+    g_down = [Gather(down_b, "x", (0, half)), Gather(down_b, "y", (half, half))]
+    w_gate, w_up = Gather(gate_b, "x"), Gather(up_b, "y")
     for g in g_in:
         g.ring_one()
-    swap_out = copy(out_weight, out_b.at[z, y, k], mirror)
-    swap_down = copy(down_weight, down_b.at[z, y, k], mirror)
+    got_x = gather_z(x_g) + gather_z(gains)
+
+    slot = lax.broadcasted_iota(jnp.int32, (slots, 1), 0)
+    count = run_counts[row]
+    offset = total([jnp.where(q < row, run_counts[q], 0) for q in range(rows)])
+    position = offset + slot
+    is_live = slot < count
+    start, seq_start = 0, jnp.zeros((slots, 1), jnp.int32)
+    for q in range(seq_lengths.shape[0]):
+        seq_start = jnp.maximum(seq_start, jnp.where(position >= start, start, 0))
+        start = start + seq_lengths[q]
+    valid1 = is_live & (position - 1 >= seq_start)
+    valid2 = is_live & (position - 2 >= seq_start)
+
+
+    def last_two(values):
+        one = jnp.sum(jnp.where(slot == count - 2, values, 0.0), axis=0, keepdims=True)
+        two = jnp.sum(jnp.where(slot == count - 1, values, 0.0), axis=0, keepdims=True)
+        return one, two
+
+    tail_s[...] = jnp.zeros(tail_s.shape, f32)
+    tail_s[0:1, :], tail_s[1:2, :] = last_two(x_g[z].astype(f32))
+    got_tail = launch(tail_s, tail_g.at[z], next_row)
+    swap_out = copy(out_i, out_b.at[z, y, k], mirror)
+    swap_down = copy(down_i, down_b.at[z, y, k], mirror)
 
     @pl.when(x != z)
     def _():
@@ -236,64 +261,68 @@
 
     @pl.when(x == z)
     def _():
-        out_b[x, y, k] = out_weight[...]
-        down_b[x, y, k] = down_weight[...]
+        out_b[x, y, k] = out_i[...]
+        down_b[x, y, k] = down_i[...]
 
     for g in g_in:
         g.ring_two()
+    got_tail.wait_recv()
+    got_tail = gather_z(tail_g)
 
     @pl.when(x != z)
     def _():
         swap_out.wait_recv()
         swap_down.wait_recv()
 
-    half = width // 2
-    g_out = [Gather(out_b, "x", (0, half)), Gather(out_b, "y", (half, half))]
-    g_down = [Gather(down_b, "x", (0, half)), Gather(down_b, "y", (half, half))]
-    w_gate, w_up = Gather(gate_b, "x"), Gather(up_b, "y")
-    for g in g_out:
-        g.ring_one()
+    g_out.ring_one()
     w_gate.ring_one()
     w_up.ring_one()
+    for g in g_down:
+        g.ring_one()
+    cot_g[z] = jnp.where(is_live, cot_g[z].astype(f32), 0.0).astype(bf16)
     got_cot = gather_z(cot_g)
 
     arrive(got_x)
+    g_out.ring_two()
     features = SIDE * width
-    squares = total([jnp.sum(jnp.square(x_g[i].astype(f32)), axis=1, keepdims=True) for i in range(SIDE)])
-    rs1_s[...] = lax.rsqrt(squares / features + epsilon)
+
+    def scale(values):
+        return lax.rsqrt(total([jnp.sum(jnp.square(v), axis=1, keepdims=True) for v in values]) / features + epsilon)
+
+    rs1_s[...] = scale([x_g[i].astype(f32) for i in range(SIDE)])
     for i in range(SIDE):
         h = ((x_g[i].astype(f32) * rs1_s[...]) * gains[i, 0:1, :]).astype(bf16)
-        h1[:, i * width : (i + 1) * width] = h
+        h1[0:slots, i * width : (i + 1) * width] = h
     for g in g_in:
         g.core()
-    for g in g_out:
-        g.ring_two()
     w_gate.ring_two()
     w_up.ring_two()
     for g in g_down:
-        g.ring_one()
+        g.ring_two()
+    arrive(got_tail)
+    tail_scale = scale([tail_g[i] for i in range(SIDE)])
     for i in range(SIDE):
-        h1_t[i] = h1[:, i * width : (i + 1) * width].T
+        h = (tail_g[i] * tail_scale) * gains[i, 0:1, :]
+        h = jnp.concatenate([h, jnp.zeros(h.shape, f32)], axis=0).astype(bf16)
+        h1[slots : slots + 16, i * width : (i + 1) * width] = h
+    for i in range(SIDE):
+        h1_t[i] = h1[0:slots, i * width : (i + 1) * width].T
 
     for g in g_in:
         g.done()
-    for p, ref in enumerate((b_s, c_s, x_s)):
-        w = in_b[:, :, :, :, p * width : (p + 1) * width].reshape(features, width)
-        ref[...] = dot(h1[...], w)
-    u = (b_s[...] * x_s[...]).astype(bf16).astype(f32)
-    halo_s[...] = jnp.zeros(halo_s.shape, f32)
-    halo_s[0:1, :] = jnp.sum(jnp.where(slot == count - 2, u, 0.0), axis=0, keepdims=True)
-    halo_s[1:2, :] = jnp.sum(jnp.where(slot == count - 1, u, 0.0), axis=0, keepdims=True)
-    got_halo = launch(halo_s, halo_r, next_row)
-    for g in g_out:
-        g.core()
+
+    def in_part(p, tokens_of):
+        return dot(tokens_of, in_b[:, :, :, :, p * width : (p + 1) * width].reshape(features, width))
+
+    b_all, x_all = in_part(0, h1[...]), in_part(2, h1[...])
+    b_s[...], x_s[...] = b_all[0:slots], x_all[0:slots]
+    c_s[...] = in_part(1, h1[0:slots, :])
+    u_all = (b_all * x_all).astype(bf16).astype(f32)
+    u, halo = u_all[0:slots], u_all[slots : slots + 8]
+    g_out.core()
     taps = conv_weight[...].astype(f32)
     tap1 = pltpu.roll(u, 1, 0)
     tap2 = pltpu.roll(u, 2, 0)
-    for g in g_out:
-        g.done()
-    got_halo.wait_recv()
-    halo = halo_r[...]
     tap1 = jnp.where(valid1, jnp.where(slot == 0, halo[1:2], tap1), 0.0)
     tap2 = jnp.where(valid2, jnp.where(slot == 0, halo[0:1], jnp.where(slot == 1, halo[1:2], tap2)), 0.0)
     tap1_s[...] = tap1
@@ -302,15 +331,14 @@
     conv_s[...] = conv
     mixed = (c_s[...] * conv).astype(bf16)
     z_t[...] = mixed.T
+    g_out.done()
 
     got_o = []
     for d in RING:
         i = wrap(z + d)
         o_s[i] = dot(mixed, out_b[i].reshape(width, width)).astype(bf16)
         got_o.append(launch(o_s.at[i], o_r.at[z], z_peer(d)))
-    r1_s[...] = tokens[...].astype(f32) + dot(mixed, out_b[z].reshape(width, width))
-    for g in g_down:
-        g.ring_two()
+    r1_s[...] = x_g[z].astype(f32) + dot(mixed, out_b[z].reshape(width, width))
     arrive(got_o)
     r1 = r1_s[...] + total([o_r[wrap(z + d)].astype(f32) for d in RING])
     r1_s[...] = r1
@@ -328,8 +356,7 @@
     g_hid[...] = total([dot_nt(cot_g[i], down_b[i].reshape(units, width)) for i in range(SIDE)])
 
     arrive(got_r1)
-    squares = total([jnp.sum(jnp.square(r1_g[i].astype(f32)), axis=1, keepdims=True) for i in range(SIDE)])
-    rs2 = lax.rsqrt(squares / features + epsilon)
+    rs2 = scale([r1_g[i].astype(f32) for i in range(SIDE)])
     for i in range(SIDE):
         h = ((r1_g[i].astype(f32) * rs2) * gains[i, 1:2, :]).astype(bf16)
         h2[:, i * width : (i + 1) * width] = h
@@ -419,6 +446,10 @@
     back_s[0:1, :] = into2[0:1, :]
     back_s[1:2, :] = into1[0:1, :] + into2[1:2, :]
     got_back = launch(back_s, back_r, last_row)
+    for i in range(SIDE):
+        out_p[i] = dot(z_t[...], go[i]).astype(bf16).reshape(out_p.shape[1:])
+    s_out = Scatter(out_p, out_1, [(out_2, "y", (0, width))], out_3)
+    s_out.core()
     vec_a[1:2, :] = jnp.sum(g_v * u, axis=0, keepdims=True)
     vec_a[2:3, :] = jnp.sum(g_v * tap1_s[...], axis=0, keepdims=True)
     vec_a[3:4, :] = jnp.sum(g_v * tap2_s[...], axis=0, keepdims=True)
@@ -455,12 +486,9 @@
     own_s[...] = part
     dots[z] = total(along) + one
     got_gh1 += gather_z(dots)
+    s_down.ring_two()
     s_in.ring_one()
-
-    for i in range(SIDE):
-        out_p[i] = dot(z_t[...], go[i]).astype(bf16).reshape(out_p.shape[1:])
-    s_out = Scatter(out_p, out_1, [(out_2a, "x", (0, half)), (out_2b, "y", (half, half))], out_3)
-    s_out.core()
+    s_out.ring_one()
 
     got_ffo = []
     for d in RING:
@@ -469,15 +497,13 @@
         got_ffo.append(launch(ffo_s.at[i], ffo_r.at[z], z_peer(d)))
     ffo_own[...] = r1_s[...] + dot(hid[...], down_b[z].reshape(units, width))
 
-    s_down.ring_two()
-    s_out.ring_one()
     s_gate.ring_two()
     s_up.ring_two()
 
     arrive(got_gh1)
     gh1 = own_s[...] + total([gh1_r[wrap(z + d)].astype(f32) for d in RING])
     mean1 = total([dots[i] for i in range(SIDE)]).T[:, 0:1] / features
-    n1 = tokens[...].astype(f32) * rs1_s[...]
+    n1 = x_g[z].astype(f32) * rs1_s[...]
     input_grad[...] = gr1_s[...] + rs1_s[...] * (gh1 * gains[z, 0:1, :] - n1 * mean1)
     vec_a[4:5, :] = jnp.sum(gh1 * n1, axis=0, keepdims=True)
     got_vec = launch(vec_a, vec_b, sibling)
@@ -537,6 +563,16 @@
     for c in started:
         if not any(c is m for m in mirrored):
             c.wait_send()
+
+
+def passing(*refs):
+    n = len(refs) // 2
+    sems = refs[-1]
+    copies = [pltpu.make_async_copy(refs[i], refs[n + i], sems.at[i]) for i in range(n)]
+    for c in copies:
+        c.start()
+    for c in copies:
+        c.wait()
 
 
 def body(
@@ -575,7 +611,7 @@
     twos = [
         vm(SIDE, SIDE, r, w)
         for r, w in (
-            (wide, three // 2), (wide, three // 2), (wide, width // 2), (wide, width // 2),
+            (wide, three // 2), (wide, three // 2), (wide, width),
             (wide, units), (wide, units), (deep, width // 2), (deep, width // 2),
         )
     ]
@@ -583,30 +619,35 @@
         vm(SIDE, r, w)
         for r, w in ((wide, three), (wide, width), (wide, units), (wide, units), (deep, width))
     ]
-    turned = [vm(wide, width, dtype=f32), vm(deep, width, dtype=f32)]
+    turned = [vm(wide, width, dtype=f32), vm(deep, width, dtype=f32), vm(wide, width), vm(deep, width)]
     own = [
-        vm(slots, features), vm(slots, features), vm(SIDE, width, slots), vm(SIDE, width, slots),
+        vm(slots + 16, features), vm(slots, features), vm(SIDE, width, slots), vm(SIDE, width, slots),
         vm(slots, units), vm(units, slots), vm(slots, units), vm(slots, units),
         vm(slots, units, dtype=f32), vm(slots, three), vm(width, slots), vm(SIDE, slots, width),
     ]
     own += [vm(slots, width, dtype=f32) for _ in range(10)] + [vm(slots, 1, dtype=f32)]
-    small = [vm(8, width, dtype=f32) for _ in range(6)] + [vm(SIDE, 8, width, dtype=f32) for _ in range(2)]
+    small = [vm(8, width, dtype=f32) for _ in range(5)] + [vm(SIDE, 8, width, dtype=f32) for _ in range(3)]
     scratch = gathered + by_col + summed + gathered + ones + twos + threes + turned + own + small
-    scratch += [pltpu.SemaphoreType.DMA((COPIES,)), pltpu.SemaphoreType.DMA((COPIES,))]
+    scratch += [pltpu.SemaphoreType.DMA((COPIES,)), pltpu.SemaphoreType.DMA((COPIES,)), pltpu.SemaphoreType.DMA((9,))]
 
     vmem, smem = pl.BlockSpec(memory_space=pltpu.VMEM), pl.BlockSpec(memory_space=pltpu.SMEM)
+    anywhere = pl.BlockSpec(memory_space=pltpu.HBM)
+
+    def hbm(array):
+        return pltpu.with_memory_space_constraint(array, pltpu.HBM)
 
     def out(*shape, dtype=f32):
         return jax.ShapeDtypeStruct(shape, dtype)
 
-    (block_out, input_grad, first_grad, in_grad, conv_grad, out_grad, second_grad, gate_grad, up_grad, down_grad) = (
+    shapes = (
+        out(slots, width, dtype=bf16), out(slots, width), out(1, width), out(3, wide, width), out(3, width),
+        out(wide, width), out(1, width), out(wide, units), out(wide, units), out(deep, width),
+    )
+    results = (
         pl.pallas_call(
             kernel,
-            out_shape=(
-                out(slots, width, dtype=bf16), out(slots, width), out(1, width), out(3, wide, width), out(3, width),
-                out(wide, width), out(1, width), out(wide, units), out(wide, units), out(deep, width),
-            ),
-            in_specs=[vmem, smem, smem] + [vmem] * 9,
+            out_shape=tuple(pltpu.VMEM(a.shape, a.dtype) for a in shapes),
+            in_specs=[anywhere, smem, smem, vmem, anywhere, vmem, anywhere, vmem] + [anywhere] * 4,
             out_specs=(vmem,) * 10,
             scratch_shapes=scratch,
             compiler_params=pltpu.CompilerParams(
@@ -614,10 +655,19 @@
             ),
             name="block",
         )(
-            tokens, run_counts, seq_lengths, first_gain.reshape(1, width), in_weight.transpose(1, 0, 2), conv_weight,
-            out_weight, second_gain.reshape(1, width), gate_weight, up_weight, down_weight, cotangent,
+            hbm(tokens), run_counts, seq_lengths, first_gain, hbm(in_weight.transpose(1, 0, 2)), conv_weight,
+            hbm(out_weight), second_gain, hbm(gate_weight), hbm(up_weight), hbm(down_weight), hbm(cotangent),
         )
     )
+    results = pl.pallas_call(
+        passing,
+        out_shape=shapes,
+        in_specs=[vmem] * 10,
+        out_specs=(anywhere,) * 10,
+        scratch_shapes=[pltpu.SemaphoreType.DMA((10,))],
+        name="results",
+    )(*(pltpu.with_memory_space_constraint(r, pltpu.VMEM) for r in results))
+    block_out, input_grad, first_grad, in_grad, conv_grad, out_grad, second_grad, gate_grad, up_grad, down_grad = results
     return (
         block_out,
         input_grad,

time: 128 us -> 114 us (0.89)
  local copies, waits for them, and re-layouts: 9.84 us -> 0 us
  Pallas kernels: 118 us -> 114 us
    unnamed x32 -> x0, local copies, waits for them, and re-layouts: 8.71 us -> none
    pallas_call x1 -> x2, Pallas kernels: 118 us -> 114 us  [the longest x1 113 us: body(): pl.pallas_call(kernel, out_shape=tuple((pltpu.VMEM(a.shape, a.dtype) for...]
where the time goes in v2:
time: 114 us
  Pallas kernels  114 us (100%)
    pallas_call x1, Pallas kernels, body(): pl.pallas_call(kernel, out_shape=tuple((pltpu.VMEM(a.shape, a.dtype) for...  113 us

profile of v2, /device:TPU:0, one launch (start us, length us, event | category | flops | bytes accessed | tf_op | source)
XLA Modules:
  0.0 114.2 jit_solution(12791975883983258887)
XLA Ops:
  0.6 112.5 %block.1 = (bf16[256,256]{1,0:T(8,128)(2,1)S(1)}, f32[256,256]{1,0:T(8,128)S(1)}, f32[1,256]{1,0:T(1,128)S(1)}, f32[3,32,256]{2,1,0:T(8,128)S(1)}, f32[3,256]{1,...) custom-call(bf16[256,256]{1,0:T(8,128)(2,1)} %tokens.1, ...), custom_call_target="tpu_custom_call" | custom-call | tf_op jit(solution)/shard_map/block/pallas_call | solution.py:647
  113.2 1.0 results.1

commit v3 on v2

--- a/solution.py
+++ b/solution.py
@@ -42,6 +42,7 @@
     in_p, out_p, gate_p, up_p, down_p,
     in_1, out_1, gate_1, up_1, down_1,
     in_2a, in_2b, out_2, gate_2, up_2, down_2a, down_2b,
+    gate_v, up_v, down_va, down_vb,
     in_3, out_3, gate_3, up_3, down_3,
     out_t, down_t, out_i, down_i,
     h1, h2, h1_t, h2_t, hid, hid_t, g_gate_ref, g_up, g_hid, g_proj, z_t, go,
@@ -136,8 +137,8 @@
         return [launch(buf.at[z], buf.at[z], z_peer(d)) for d in RING]
 
     class Gather:
-        def __init__(self, buf, first, cols=None):
-            self.buf, self.first = buf, first
+        def __init__(self, buf, first, cols=None, relayed=False):
+            self.buf, self.first, self.relayed = buf, first, relayed
             self.cols = slice(None) if cols is None else pl.ds(*cols)
 
         def ring_one(self):
@@ -151,7 +152,18 @@
                 part, peer = self.buf.at[:, y, k, :, self.cols], y_peer
             else:
                 part, peer = self.buf.at[x, :, k, :, self.cols], x_peer
-            self.pending = [launch(part, part, peer(d)) for d in RING]
+            self.pending = [launch(part, part, peer(d)) for d in (RING[:2] if self.relayed else RING)]
+
+        def relay(self):
+            arrive(self.pending)
+            low, high = slice(0, SIDE // 2), slice(SIDE // 2, SIDE)
+            if self.first == "x":
+                up, down = self.buf.at[low, wrap(y + 3), k, :, self.cols], self.buf.at[high, wrap(y + 1), k, :, self.cols]
+                peer = y_peer
+            else:
+                up, down = self.buf.at[wrap(x + 3), low, k, :, self.cols], self.buf.at[wrap(x + 1), high, k, :, self.cols]
+                peer = x_peer
+            self.pending = [launch(up, up, peer(1)), launch(down, down, peer(3))]
 
         def core(self):
             arrive(self.pending)
@@ -220,12 +232,69 @@
             arrive(self.pending)
             return total([self.three[s].astype(f32) for s in range(SIDE)])
 
+    class Relay(Scatter):
+        def ring_one(self):
+            arrive(self.pending)
+            one, partial = self.one, self.partial
+
+            @pl.loop(0, SIDE * SIDE)
+            def _(i):
+                a, b = i // SIDE, wrap(i)
+                one[a, b] = (partial[a, b, k].astype(f32) + one[a, b].astype(f32)).astype(bf16)
+
+            low, high = slice(0, SIDE // 2), slice(SIDE // 2, SIDE)
+            self.pending = []
+            for two, via, first, cols in self.parts:
+                cs = pl.ds(*cols)
+                if first == "x":
+                    far = wrap(x + 2)
+                    up, down, peer = one.at[far, low, :, cs], one.at[far, high, :, cs], x_peer
+                else:
+                    far = wrap(y + 2)
+                    up, down, peer = one.at[low, far, :, cs], one.at[high, far, :, cs], y_peer
+                self.pending.append([launch(up, via.at[0], peer(1)), launch(down, via.at[1], peer(3))])
+
+        def relay(self):
+            one, later = self.one, []
+            for (two, via, first, cols), sent in zip(self.parts, self.pending):
+                arrive(sent)
+                cs = pl.ds(*cols)
+                for j in range(SIDE // 2):
+                    if first == "x":
+                        a, b = (wrap(x + 1), j), (wrap(x + 3), j + SIDE // 2)
+                    else:
+                        a, b = (j, wrap(y + 1)), (j + SIDE // 2, wrap(y + 3))
+                    for n, at_n in ((0, a), (1, b)):
+                        both = one[at_n[0], at_n[1], :, cs].astype(f32) + via[n, j].astype(f32)
+                        one[at_n[0], at_n[1], :, cs] = both.astype(bf16)
+                if first == "x":
+                    up, down, peer = one.at[wrap(x + 1), :, :, cs], one.at[wrap(x + 3), :, :, cs], x_peer
+                else:
+                    up, down, peer = one.at[:, wrap(y + 1), :, cs], one.at[:, wrap(y + 3), :, cs], y_peer
+                later.append([launch(up, two.at[0], peer(1)), launch(down, two.at[1], peer(3))])
+            self.pending = later
+
+        def ring_two(self):
+            one, later = self.one, []
+            for (two, via, first, cols), sent in zip(self.parts, self.pending):
+                arrive(sent)
+                cs = pl.ds(*cols)
+                for j in range(SIDE):
+                    own = one[x, j, :, cs] if first == "x" else one[j, y, :, cs]
+                    two[0, j] = (own.astype(f32) + two[0, j].astype(f32) + two[1, j].astype(f32)).astype(bf16)
+                to = y if first == "x" else x
+                peer = y_peer if first == "x" else x_peer
+                for d in RING:
+                    later.append(launch(two.at[0, wrap(to + d)], self.three.at[to, :, cs], peer(d)))
+                self.three[to, :, cs] = two[0, to]
+            self.pending = later
+
     in_half = in_b.shape[-1] // 2
     half = width // 2
     g_in = [Gather(in_b, "x", (0, in_half)), Gather(in_b, "y", (in_half, in_half))]
     g_out = Gather(out_b, "x")
-    g_down = [Gather(down_b, "x", (0, half)), Gather(down_b, "y", (half, half))]
-    w_gate, w_up = Gather(gate_b, "x"), Gather(up_b, "y")
+    g_down = [Gather(down_b, "x", (0, half), True), Gather(down_b, "y", (half, half), True)]
+    w_gate, w_up = Gather(gate_b, "x", None, True), Gather(up_b, "y", None, True)
     for g in g_in:
         g.ring_one()
     got_x = gather_z(x_g) + gather_z(gains)
@@ -284,6 +353,10 @@
 
     arrive(got_x)
     g_out.ring_two()
+    w_gate.ring_two()
+    w_up.ring_two()
+    for g in g_down:
+        g.ring_two()
     features = SIDE * width
 
     def scale(values):
@@ -295,10 +368,6 @@
         h1[0:slots, i * width : (i + 1) * width] = h
     for g in g_in:
         g.core()
-    w_gate.ring_two()
-    w_up.ring_two()
-    for g in g_down:
-        g.ring_two()
     arrive(got_tail)
     tail_scale = scale([tail_g[i] for i in range(SIDE)])
     for i in range(SIDE):
@@ -344,16 +413,17 @@
     r1_s[...] = r1
     r1_g[z] = r1.astype(bf16)
     got_r1 = gather_z(r1_g)
+    w_gate.relay()
+    w_up.relay()
+    for g in g_down:
+        g.relay()
 
     arrive(got_cot)
     w_gate.core()
     w_up.core()
     for g in g_down:
         g.core()
-    for g in g_down:
-        g.done()
     units = hid.shape[1]
-    g_hid[...] = total([dot_nt(cot_g[i], down_b[i].reshape(units, width)) for i in range(SIDE)])
 
     arrive(got_r1)
     rs2 = scale([r1_g[i].astype(f32) for i in range(SIDE)])
@@ -363,6 +433,9 @@
 
     w_gate.done()
     w_up.done()
+    for g in g_down:
+        g.done()
+    g_hid[...] = total([dot_nt(cot_g[i], down_b[i].reshape(units, width)) for i in range(SIDE)])
     tile = units // 3
     for n in range(3):
         cs = slice(n * tile, (n + 1) * tile)
@@ -393,7 +466,7 @@
     def _(i):
         down_p[i] = dot(hid_t[...], cot_g[i]).astype(bf16).reshape(down_p.shape[1:])
 
-    s_down = Scatter(down_p, down_1, [(down_2a, "x", (0, half)), (down_2b, "y", (half, half))], down_3)
+    s_down = Relay(down_p, down_1, [(down_2a, down_va, "x", (0, half)), (down_2b, down_vb, "y", (half, half))], down_3)
     s_down.core()
     for i in range(SIDE):
         h2_t[i] = h2[:, i * width : (i + 1) * width].T
@@ -402,7 +475,7 @@
     def _(i):
         gate_p[i] = dot(h2_t[i], g_gate_ref[...]).astype(bf16).reshape(gate_p.shape[1:])
 
-    s_gate = Scatter(gate_p, gate_1, [(gate_2, "x", (0, units))], gate_3)
+    s_gate = Relay(gate_p, gate_1, [(gate_2, gate_v, "x", (0, units))], gate_3)
     s_gate.core()
     arrive(got_gh2)
     gh2_g[z] = (own_s[...] + total([gh2_r[wrap(z + d)].astype(f32) for d in RING])).astype(bf16)
@@ -413,12 +486,19 @@
     def _(i):
         up_p[i] = dot(h2_t[i], g_up[...]).astype(bf16).reshape(up_p.shape[1:])
 
-    s_up = Scatter(up_p, up_1, [(up_2, "y", (0, units))], up_3)
+    s_up = Relay(up_p, up_1, [(up_2, up_v, "y", (0, units))], up_3)
     s_up.core()
     s_gate.ring_one()
     s_up.ring_one()
+    s_down.relay()
+
+    for d in RING:
+        i = wrap(z + d)
+        ffo_s[i] = dot(hid[...], down_b[i].reshape(units, width)).astype(bf16)
+    ffo_own[...] = r1_s[...] + dot(hid[...], down_b[z].reshape(units, width))
 
     arrive(got_gh2)
+    got_ffo = [launch(ffo_s.at[wrap(z + d)], ffo_r.at[z], z_peer(d)) for d in RING]
     mean2 = total(
         [
             jnp.sum(gh2_g[i].astype(f32) * gains[i, 1:2, :] * (r1_g[i].astype(f32) * rs2), axis=1, keepdims=True)
@@ -467,6 +547,8 @@
         in_p[i] = dot(h1_t[i], g_proj[...]).astype(bf16).reshape(in_p.shape[1:])
     s_in = Scatter(in_p, in_1, [(in_2a, "x", (0, in_half)), (in_2b, "y", (in_half, in_half))], in_3)
     s_in.core()
+    s_gate.relay()
+    s_up.relay()
 
     ones = jnp.ones((8, width), bf16)
 
@@ -486,16 +568,9 @@
     own_s[...] = part
     dots[z] = total(along) + one
     got_gh1 += gather_z(dots)
-    s_down.ring_two()
     s_in.ring_one()
     s_out.ring_one()
-
-    got_ffo = []
-    for d in RING:
-        i = wrap(z + d)
-        ffo_s[i] = dot(hid[...], down_b[i].reshape(units, width)).astype(bf16)
-        got_ffo.append(launch(ffo_s.at[i], ffo_r.at[z], z_peer(d)))
-    ffo_own[...] = r1_s[...] + dot(hid[...], down_b[z].reshape(units, width))
+    s_down.ring_two()
 
     s_gate.ring_two()
     s_up.ring_two()
@@ -608,13 +683,9 @@
         vm(SIDE, SIDE, r, w)
         for r, w in ((wide, three), (wide, width), (wide, units), (wide, units), (deep, width))
     ]
-    twos = [
-        vm(SIDE, SIDE, r, w)
-        for r, w in (
-            (wide, three // 2), (wide, three // 2), (wide, width),
-            (wide, units), (wide, units), (deep, width // 2), (deep, width // 2),
-        )
-    ]
+    twos = [vm(SIDE, SIDE, wide, w) for w in (three // 2, three // 2, width)]
+    relayed = ((wide, units), (wide, units), (deep, width // 2), (deep, width // 2))
+    twos += [vm(2, SIDE, r, w) for r, w in relayed] + [vm(2, SIDE // 2, r, w) for r, w in relayed]
     threes = [
         vm(SIDE, r, w)
         for r, w in ((wide, three), (wide, width), (wide, units), (wide, units), (deep, width))

time: 114 us -> 111 us (0.974)
  Pallas kernels: 114 us -> 110 us
    pallas_call x1, Pallas kernels: 113 us -> 109 us  [body(): pl.pallas_call(kernel, out_shape=tuple((pltpu.VMEM(a.shape, a.dtype) for...]
where the time goes in v3:
time: 111 us; the launch traced here: 110 us
  Pallas kernels  110 us (99%)
    pallas_call x1, Pallas kernels, body(): pl.pallas_call(kernel, out_shape=tuple((pltpu.VMEM(a.shape, a.dtype) for...  109 us

profile of v3, /device:TPU:0, one launch (start us, length us, event | category | flops | bytes accessed | tf_op | source)
XLA Modules:
  0.0 110.5 jit_solution(8914790649651566254)
XLA Ops:
  0.6 108.8 %block.1 = (bf16[256,256]{1,0:T(8,128)(2,1)S(1)}, f32[256,256]{1,0:T(8,128)S(1)}, f32[1,256]{1,0:T(1,128)S(1)}, f32[3,32,256]{2,1,0:T(8,128)S(1)}, f32[3,256]{1,...) custom-call(bf16[256,256]{1,0:T(8,128)(2,1)} %tokens.1, ...), custom_call_target="tpu_custom_call" | custom-call | tf_op jit(solution)/shard_map/block/pallas_call | solution.py:718
  109.4 1.0 results.1
